TPU v7x, 128 devices: a whole 4x4x4 slice. The times are simulated.
128 devices in a mesh: wide: 16 (over z, x), narrow: 8 (over y, core).
Axes of the slice: x: 4, y: 4, z: 4, core: 2. Of those that a mesh axis runs over, the one named last changes fastest.
Arguments:
- tokens: bfloat16 [1024, 12288], P('narrow'), may hold values from -6 to 6
- first_blocks: bfloat16 [384, 40, 128, 128], P('wide', 'narrow'), may hold values from -0.109375 to 0.109375
- second_blocks: bfloat16 [384, 40, 128, 128], P('wide', 'narrow'), may hold values from -0.0546875 to 0.0546875
- block_rows: int32 [384, 40], P('wide', 'narrow'), may hold values from 0 to 11, as said below
- block_count: int32 [384, 8], P('wide', 'narrow'), may hold values from 1 to 5, as said below
- upstream: bfloat16 [1024, 12288], P('narrow'), may hold values from -1.5 to 1.5
Outputs:
- layer_output: bfloat16 [1024, 12288], P('wide', 'narrow')
- grad_tokens: bfloat16 [1024, 12288], P('wide', 'narrow')
- first_grad: float32 [384, 40, 128, 128], P('wide', 'narrow')
- second_grad: float32 [384, 40, 128, 128], P('wide', 'narrow')
Inputs may be any that keep to these rules, and one draw needn't show every extreme that they name: `block_rows`: within each panel and each group of 5 slots the values are distinct. The first block_count slots of a panel's group are kept; in every group some panel keeps all 5.
All inputs are finite; a program needn't handle non-finite values.
Results may differ from a plain program's by a relative error of at most 0.029.
Values may be sent and summed in bfloat16 or wider, within the bound.
A program may use at most 320 MiB of HBM per device.

v0:
```python
import math
import jax
import jax.numpy as jnp
from jax import lax
from jax.sharding import PartitionSpec as P


def on_device(tokens, first_blocks, second_blocks, block_rows, block_count, upstream):
    wide_size = lax.axis_size("wide")
    narrow_size = lax.axis_size("narrow")
    panels, capacity, block_size, _ = first_blocks.shape
    width_total = tokens.shape[1]
    group_blocks = width_total // narrow_size // block_size
    kept_mask = jnp.arange(capacity, dtype=jnp.int32)[None, :] < block_count
    kept_blocks = kept_mask[:, :, None, None]
    first_kept = jnp.where(kept_blocks, first_blocks, jnp.zeros((), jnp.bfloat16))
    second_kept = jnp.where(kept_blocks, second_blocks, jnp.zeros((), jnp.bfloat16))
    block_selector = (
        block_rows[:, :, None] == jnp.arange(group_blocks, dtype=jnp.int32)[None, None, :]
    ).astype(jnp.bfloat16)
    token_all, upstream_all = (
        lax.all_to_all(tokens, "narrow", split_axis=1, concat_axis=0, tiled=True),
        lax.all_to_all(upstream, "narrow", split_axis=1, concat_axis=0, tiled=True),
    )
    token_count = token_all.shape[0]
    token_slots = jnp.take(
        token_all.reshape(token_count, group_blocks, block_size), block_rows, axis=1
    )
    upstream_slots = jnp.take(
        upstream_all.reshape(token_count, group_blocks, block_size), block_rows, axis=1
    )

    def hidden_sum(slots, weight_matrices, pattern):
        product = jnp.einsum(pattern, slots, weight_matrices, preferred_element_type=jnp.float32)
        return lax.psum_scatter(
            product.reshape(
                lax.axis_size("narrow") * (token_count // narrow_size), panels * block_size
            ).astype(jnp.bfloat16),
            "narrow",
            scatter_dimension=0,
            tiled=True,
        ).astype(jnp.float32)

    def hidden_rows(share):
        return lax.all_gather(share, "narrow", axis=0, tiled=True)

    def width_sum(source, weight_matrices, pattern):
        amount = lax.axis_size("wide") * (token_count // wide_size)
        row_segment = source.reshape(amount, panels, block_size)
        step_rows = math.gcd(amount, 512)

        def apply_block(rows_block):
            product = jnp.einsum(
                pattern, rows_block, weight_matrices, preferred_element_type=jnp.float32
            )
            upper_bound = product.astype(jnp.bfloat16)
            lower_bound = (product - upper_bound.astype(jnp.float32)).astype(jnp.bfloat16)
            placed = jnp.einsum(
                "svob,voy->syb", upper_bound, block_selector, preferred_element_type=jnp.float32
            )
            placed = placed + jnp.einsum(
                "svob,voy->syb", lower_bound, block_selector, preferred_element_type=jnp.float32
            )
            return placed.reshape(step_rows, group_blocks * block_size)

        results = lax.map(
            apply_block, row_segment.reshape(amount // step_rows, step_rows, panels, block_size)
        )
        return lax.psum_scatter(
            results.reshape(amount, group_blocks * block_size).astype(jnp.bfloat16),
            "wide",
            scatter_dimension=0,
            tiled=True,
        ).astype(jnp.float32)

    preact = hidden_sum(token_slots, first_kept, "tpck,pckf->tpf")
    hidden_portion = jax.nn.gelu(preact).astype(jnp.bfloat16)
    hidden_all = hidden_rows(hidden_portion)
    layer_output = width_sum(hidden_all, second_kept, "tpf,pcfk->tpck").astype(jnp.bfloat16)
    hidden_gradient = hidden_sum(upstream_slots, second_kept, "tpck,pcfk->tpf")
    pullback = jax.vjp(jax.nn.gelu, preact)[1]
    grad_pre = pullback(hidden_gradient)[0].astype(jnp.bfloat16)
    grad_all = hidden_rows(grad_pre)
    hidden_panels = hidden_all.reshape(token_count, panels, block_size)
    grad_panels = grad_all.reshape(token_count, panels, block_size)
    second_grad = jnp.where(
        kept_blocks,
        jnp.einsum(
            "tpf,tpck->pcfk", hidden_panels, upstream_slots, preferred_element_type=jnp.float32
        ),
        0.0,
    )
    first_grad = jnp.where(
        kept_blocks,
        jnp.einsum("tpck,tpf->pckf", token_slots, grad_panels, preferred_element_type=jnp.float32),
        0.0,
    )
    grad_tokens = width_sum(grad_all, first_kept, "tpf,pckf->tpck").astype(jnp.bfloat16)
    return (layer_output, grad_tokens, first_grad, second_grad)


def solution(mesh):
    in_specs = (
        P("narrow", None),
        P("wide", "narrow", None, None),
        P("wide", "narrow", None, None),
        P("wide", "narrow"),
        P("wide", "narrow"),
        P("narrow", None),
    )
    out_specs = (
        P("wide", "narrow"),
        P("wide", "narrow"),
        P("wide", "narrow", None, None),
        P("wide", "narrow", None, None),
    )
    return jax.shard_map(
        on_device, mesh=mesh, in_specs=in_specs, out_specs=out_specs, check_vma=False
    )
```

profile of v0, /device:TPU:0, one launch (start us, length us, event | category | flops | bytes accessed | tf_op | source)
XLA Modules:
  0.0 767.6 jit_solution(12117050786698228819)
XLA Ops:
  23.1 31.9 %all-to-all-done = bf16[128,8,1536]{0,2,1:T(8,128)(2,1)S(1)} async-done(((bf16[128,8,1536]{0,2,1:T(8,128)(2,1)}), bf16[128,8,1536]{0,2,1:T(8,128)(2,1)S(1)}, u32[]{:S(2)}, u32[]{:S(2)}) %all-to-all-start) | async-done | bytes 3145760 | tf_op jit(solution)/shard_map/all_to_all | solution.py:22
  86.5 40.8 %copy.61 = bf16[24,5,1024,128]{2,3,1,0:T(8,128)(2,1)} copy(bf16[24,5,1024,128]{3,2,1,0:T(8,128)(2,1)} %bitcast.162) | data formatting | bytes 62914560 | tf_op jit(solution)/shard_map/jit(_take)/gather | solution.py:26
  127.3 16.1 %bitcast_convert_fusion.3 = bf16[24,128,1024]{2,1,0:T(8,128)(2,1)} fusion(bf16[24,5,128,128]{3,2,1,0:T(8,128)(2,1)} %get-tuple-element.238, bf16[24,5,1024,128]{2,3,1,0:T(8,128)(2,1)} %copy.61, pred[24,5]{1,0:T(8,128)(4,1)S(1)} %copy.56), kind=kOutput, calls=%fused_computation.57 | convolution fusion | flops 4045406208 | bytes 41681016 | tf_op jit(solution)/shard_map/tpck,pckf->tpf/dot_general | solution.py:34
  155.6 57.4 %all_to_all.32 = bf16[128,8,1536]{0,2,1:T(8,128)(2,1)S(1)} all-to-all(bf16[128,8,1536]{0,2,1:T(8,128)(2,1)S(1)} %bitcast.170), channel_id=1, replica_groups=mesh['wide'=16,'narrow'=8] {'narrow'}, dimensions={1} | all-to-all | bytes 6291456 | tf_op jit(solution)/shard_map/all_to_all | solution.py:23
  241.0 40.7 %copy.72 = bf16[24,5,1024,128]{2,3,1,0:T(8,128)(2,1)} copy(bf16[24,5,1024,128]{3,2,1,0:T(8,128)(2,1)} %bitcast.161) | data formatting | bytes 62914560 | tf_op jit(solution)/shard_map/jit(_take)/gather | solution.py:29
  281.7 16.4 %bitcast_convert_fusion.2 = bf16[24,128,1024]{2,1,0:T(8,128)(2,1)} fusion(bf16[24,5,128,128]{3,2,1,0:T(8,128)(2,1)} %get-tuple-element.220, bf16[24,5,1024,128]{2,3,1,0:T(8,128)(2,1)} %copy.72, pred[24,5]{1,0:T(8,128)(4,1)S(1)} %copy.56), kind=kOutput, calls=%fused_computation.56 | convolution fusion | flops 4045406208 | bytes 41681016 | tf_op jit(solution)/shard_map/tpck,pcfk->tpf/dot_general | solution.py:34
  308.3 41.7 %reduce-scatter.15.cloned.1.call-done = bf16[128,3072]{1,0:T(8,128)(2,1)} async-done(((bf16[1024,3072]{1,0:T(8,128)(2,1)}), bf16[128,3072]{1,0:T(8,128)(2,1)}) %reduce-scatter.15.cloned.1.call-update) | async-done | bytes 786448
  354.6 44.2 %all-gather.5.cloned.1.call-done = bf16[1024,3072]{0,1:T(8,128)(2,1)} async-done(((bf16[128,3072]{0,1:T(8,128)(2,1)}), bf16[1024,3072]{0,1:T(8,128)(2,1)}) %all-gather.5.cloned.1.call-update) | async-done | bytes 6291472 | tf_op jit(solution)/shard_map/all_gather | solution.py:45
  409.9 16.4 %copy.75 = bf16[2,512,24,128]{3,1,2,0:T(8,128)(2,1)} copy(bf16[2,512,24,128]{1,0,3,2:T(2,128)(2,1)} %reshape.113) | data formatting | bytes 12582912
  428.2 101.8 %while.23 = (s32[]{:T(128)}, bf16[2,512,1536]{1,2,0:T(8,128)(2,1)}, bf16[2,512,24,128]{3,1,2,0:T(8,128)(2,1)}, bf16[24,5,128,128]{3,2,1,0:T(8,128)(2,1)}, s32[24,5]{0,1:T(8,128)S(1)}, /*index=5*/s32[]{:T(128)}) while((s32[]{:T(128)}, bf16[2,512,1536]{1,2,0:T(8,128)(2,1)}, bf16[2,512,24,128]{3,1,2,0:T(8,128)(2,1)}, ...), condition=%wide.region_6.8_spmd.clone, body=%wide.region_5.7_spmd.clone.sunk | while | flops 2423789056 | bytes 84150280 | solution.py:66
  443.4 15.9 %fusion.111 = f32[512,128,12,1]{1,2,3,0:T(8,128)S(1)} fusion(bf16[512,24,5,128]{3,0,2,1:T(8,128)(2,1)} %get-tuple-element.215, s32[24,5]{0,1:T(8,128)S(1)} %get-tuple-element.251), kind=kOutput, calls=%fused_computation.26.clone.1 | convolution fusion | flops 188746560 | bytes 18874848 | tf_op jit(solution)/shard_map/while/body/eval_jaxpr/svob,voy->syb/dot_general | solution.py:61
  459.3 15.6 %fusion.112 = bf16[512,12,128]{2,1,0:T(8,128)(2,1)} fusion(f32[512,128,12,1]{1,2,3,0:T(8,128)S(1)} %fusion.111, bf16[512,24,5,128]{3,0,2,1:T(8,128)(2,1)} %get-tuple-element.216, s32[24,5]{0,1:T(8,128)S(1)} %get-tuple-element.251), kind=kOutput, calls=%fused_computation.31.clone.1 | convolution fusion | flops 190319424 | bytes 20447712 | tf_op jit(solution)/shard_map/while/body/eval_jaxpr/svob,voy->syb/dot_general | solution.py:58
  494.2 15.6 %fusion.111 = f32[512,128,12,1]{1,2,3,0:T(8,128)S(1)} fusion(bf16[512,24,5,128]{3,0,2,1:T(8,128)(2,1)} %get-tuple-element.215, s32[24,5]{0,1:T(8,128)S(1)} %get-tuple-element.251), kind=kOutput, calls=%fused_computation.26.clone.1 | convolution fusion | flops 188746560 | bytes 18874848 | tf_op jit(solution)/shard_map/while/body/eval_jaxpr/svob,voy->syb/dot_general | solution.py:61
  509.8 15.6 %fusion.112 = bf16[512,12,128]{2,1,0:T(8,128)(2,1)} fusion(f32[512,128,12,1]{1,2,3,0:T(8,128)S(1)} %fusion.111, bf16[512,24,5,128]{3,0,2,1:T(8,128)(2,1)} %get-tuple-element.216, s32[24,5]{0,1:T(8,128)S(1)} %get-tuple-element.251), kind=kOutput, calls=%fused_computation.31.clone.1 | convolution fusion | flops 190319424 | bytes 20447712 | tf_op jit(solution)/shard_map/while/body/eval_jaxpr/svob,voy->syb/dot_general | solution.py:58
  545.9 16.2 %copy.65 = bf16[2,512,24,128]{3,1,2,0:T(8,128)(2,1)} copy(bf16[2,512,24,128]{1,0,3,2:T(2,128)(2,1)} %reshape.112) | data formatting | bytes 12582912
  563.9 114.9 %while.22 = (s32[]{:T(128)}, bf16[2,512,1536]{1,2,0:T(8,128)(2,1)}, bf16[2,512,24,128]{3,1,2,0:T(8,128)(2,1)}, bf16[24,5,128,128]{3,2,1,0:T(8,128)(2,1)}, s32[24,5]{0,1:T(8,128)S(1)}, /*index=5*/s32[]{:T(128)}) while((s32[]{:T(128)}, bf16[2,512,1536]{1,2,0:T(8,128)(2,1)}, bf16[2,512,24,128]{3,1,2,0:T(8,128)(2,1)}, ...), condition=%wide.region_2.4_spmd.clone, body=%wide.region_1.3_spmd.clone.sunk | while | flops 2423789056 | bytes 84150280 | solution.py:66
  576.4 15.4 %fusion.102 = (bf16[512,24,5,128]{3,0,2,1:T(8,128)(2,1)}, bf16[512,24,5,128]{3,0,2,1:T(8,128)(2,1)}) fusion(bf16[24,5,128,128]{3,2,1,0:T(8,128)(2,1)} %get-tuple-element.232, bf16[2,512,24,128]{3,1,2,0:T(8,128)(2,1)} %get-tuple-element.231, s32[]{:T(128)} %get-tuple-element.223), kind=kOutput, calls=%fused_computation.6.clone.1 | convolution fusion | flops 2044723200 | bytes 38535680 | tf_op jit(solution)/shard_map/while/body/eval_jaxpr/tpf,pcfk->tpck/dot_general | solution.py:53
  591.8 15.6 %fusion.103 = f32[512,128,12,1]{1,2,3,0:T(8,128)S(1)} fusion(bf16[512,24,5,128]{3,0,2,1:T(8,128)(2,1)} %get-tuple-element.208, s32[24,5]{0,1:T(8,128)S(1)} %get-tuple-element.233), kind=kOutput, calls=%fused_computation.7.clone.1 | convolution fusion | flops 188746560 | bytes 18874848 | tf_op jit(solution)/shard_map/while/body/eval_jaxpr/svob,voy->syb/dot_general | solution.py:61
  607.4 15.8 %fusion.104 = bf16[512,12,128]{2,1,0:T(8,128)(2,1)} fusion(f32[512,128,12,1]{1,2,3,0:T(8,128)S(1)} %fusion.103, bf16[512,24,5,128]{3,0,2,1:T(8,128)(2,1)} %get-tuple-element.209, s32[24,5]{0,1:T(8,128)S(1)} %get-tuple-element.233), kind=kOutput, calls=%fused_computation.12.clone.1 | convolution fusion | flops 190319424 | bytes 20447712 | tf_op jit(solution)/shard_map/while/body/eval_jaxpr/svob,voy->syb/dot_general | solution.py:58
  642.9 15.6 %fusion.103 = f32[512,128,12,1]{1,2,3,0:T(8,128)S(1)} fusion(bf16[512,24,5,128]{3,0,2,1:T(8,128)(2,1)} %get-tuple-element.208, s32[24,5]{0,1:T(8,128)S(1)} %get-tuple-element.233), kind=kOutput, calls=%fused_computation.7.clone.1 | convolution fusion | flops 188746560 | bytes 18874848 | tf_op jit(solution)/shard_map/while/body/eval_jaxpr/svob,voy->syb/dot_general | solution.py:61
  658.5 15.6 %fusion.104 = bf16[512,12,128]{2,1,0:T(8,128)(2,1)} fusion(f32[512,128,12,1]{1,2,3,0:T(8,128)S(1)} %fusion.103, bf16[512,24,5,128]{3,0,2,1:T(8,128)(2,1)} %get-tuple-element.209, s32[24,5]{0,1:T(8,128)S(1)} %get-tuple-element.233), kind=kOutput, calls=%fused_computation.12.clone.1 | convolution fusion | flops 190319424 | bytes 20447712 | tf_op jit(solution)/shard_map/while/body/eval_jaxpr/svob,voy->syb/dot_general | solution.py:58
  683.6 18.7 %select_bitcast_fusion = f32[24,5,128,128]{2,3,1,0:T(8,128)} fusion(pred[24,5]{1,0:T(8,128)(4,1)S(1)} %copy-done.3, bf16[1024,24,128,1]{0,2,3,1:T(8,128)(2,1)} %bitcast.172, bf16[24,5,1024,128]{2,3,1,0:T(8,128)(2,1)} %copy.72, pred[24,5]{1,0:T(8,128)(4,1)S(1)} %copy-done.5), kind=kOutput, calls=%fused_computation.58 | convolution fusion | flops 4044226560 | bytes 45613296 | tf_op jit(solution)/shard_map/tpf,tpck->pcfk/dot_general | solution.py:88
  711.5 18.8 %broadcast_select_fusion.6 = f32[24,5,128,128]{3,2,1,0:T(8,128)} fusion(pred[24,5]{1,0:T(8,128)(4,1)S(1)} %copy-done.3, bf16[1024,24,128,1]{0,2,3,1:T(8,128)(2,1)} %bitcast.171, bf16[24,5,1024,128]{2,3,1,0:T(8,128)(2,1)} %copy.61, pred[24,5]{1,0:T(8,128)(4,1)S(1)} %copy-done.5), kind=kOutput, calls=%fused_computation.59 | convolution fusion | flops 4044226560 | bytes 45613296 | tf_op jit(solution)/shard_map/tpck,tpf->pckf/dot_general | solution.py:95
  730.3 30.3 %reduce-scatter.9.cloned.1.call-done = bf16[64,1536]{1,0:T(8,128)(2,1)} async-done(((bf16[1024,1536]{1,0:T(8,128)(2,1)}), bf16[64,1536]{1,0:T(8,128)(2,1)}) %reduce-scatter.9.cloned.1.call-update) | async-done | bytes 196624 | tf_op jit(solution)/shard_map/reduce_scatter | solution.py:69
  (71 shorter events, 209.9 us)
Async XLA Ops:
  11.8 4.7 copy-start
  11.8 5.1 copy-start.6
  11.8 43.1 %all-to-all-start = ((bf16[128,8,1536]{0,2,1:T(8,128)(2,1)}), bf16[128,8,1536]{0,2,1:T(8,128)(2,1)S(1)}, u32[]{:S(2)}, u32[]{:S(2)}) async-start(bf16[128,8,1536]{0,2,1:T(8,128)(2,1)} %bitcast.168), calls=%async_computation | async-start | bytes 6291456 | tf_op jit(solution)/shard_map/all_to_all | solution.py:22
  16.5 290.3 %reduce-scatter.13.cloned.1.call-start = ((), (), s32[]{:S(2)}) async-start(), calls=%async_computation.10 | async-start | bytes 7077888
  16.7 265.0 %copy-start.4 = (pred[24,5]{1,0:T(8,128)(4,1)}, pred[24,5]{1,0:T(8,128)(4,1)S(1)}, u32[]{:S(2)}) copy-start(pred[24,5]{1,0:T(8,128)(4,1)S(1)} %copy.56) | copy-start | bytes 364
  17.0 0.6 copy-start.2
  152.1 197.9 %reduce-scatter.15.cloned.1.call-start = ((), (), s32[]{:S(2)}) async-start(), calls=%async_computation.11 | async-start | bytes 7077888
  306.8 92.0 %all-gather.5.cloned.1.call-start = ((), (), s32[]{:S(2)}) async-start(), calls=%async_computation.8 | async-start | bytes 7077888 | tf_op jit(solution)/shard_map/all_gather | solution.py:45
  353.9 180.8 %all-gather.3.cloned.1.call-start = ((), (), s32[]{:S(2)}) async-start(), calls=%async_computation.6 | async-start | bytes 7077888 | tf_op jit(solution)/shard_map/all_gather | solution.py:45
  354.5 375.8 %reduce-scatter.11.cloned.1.call-start = ((), (), s32[]{:S(2)}) async-start(), calls=%async_computation.9 | async-start | bytes 3342336 | tf_op jit(solution)/shard_map/reduce_scatter | solution.py:69
  409.9 18.2 %copy-start.1 = (s32[24,5]{0,1:T(8,128)S(1)}, s32[24,5]{0,1:T(8,128)}, u32[]{:S(2)}) copy-start(s32[24,5]{0,1:T(8,128)} %param.15) | copy-start | bytes 1444
  534.7 225.9 %reduce-scatter.9.cloned.1.call-start = ((), (), s32[]{:S(2)}) async-start(), calls=%async_computation.7 | async-start | bytes 3342336 | tf_op jit(solution)/shard_map/reduce_scatter | solution.py:69
  678.9 4.7 copy-start.3
  678.9 4.7 copy-start.5
Sparse Core Ops, SparseCore 0:
  152.2 74.9 reduce-scatter.12
  306.9 43.0 reduce-scatter.14
  354.1 44.6 all-gather.4
  400.3 45.9 all-gather.2
  534.8 76.7 reduce-scatter.10
  683.7 76.7 reduce-scatter.8
where the time goes:
time: 780 us; the launch traced here: 768 us
  local copies, waits for them, and re-layouts  265 us (34%)
  matrix products  256 us (33%)
  waiting for transfers between devices  149 us (19%)
  blocking collectives  57.4 us (7%)
  between operations  14.5 us (2%)
  loops' own time  13 us (2%)
  other arithmetic  8.03 us (1%)
    unnamed x23, local copies, waits for them, and re-layouts  70.7 us
    dot_general x4, matrix products, apply_block(): jnp.einsum('svob,voy->syb', lower_bound, block_selector, preferred_elemen...  62.8 us
    dot_general x4, matrix products, apply_block(): jnp.einsum('svob,voy->syb', upper_bound, block_selector, preferred_elemen...  62.6 us
    dot_general x4, matrix products, apply_block(): jnp.einsum(pattern, rows_block, weight_matrices, preferred_element_type=j...  60.3 us
    all_to_all x1, blocking collectives, on_device(): lax.all_to_all(upstream, 'narrow', split_axis=1, concat_axis=0, tiled=True)  57.4 us
    gather x2, local copies, waits for them, and re-layouts, on_device(): jnp.take(token_all.reshape(token_count, group_blocks, block_size), block_...  53 us
    gather x2, local copies, waits for them, and re-layouts, on_device(): jnp.take(upstream_all.reshape(token_count, group_blocks, block_size), blo...  53 us
    all_gather x2, waiting for transfers between devices, hidden_rows(): return lax.all_gather(share, 'narrow', axis=0, tiled=True)  44.2 us
  transfers between devices with their start and end apart: 7, of which 4 were waited for; matrix products, arithmetic and copies ran while one was open for 55% of the time, Pallas kernels for 0%

commit v1 on v0

--- a/solution.py
+++ b/solution.py
@@ -42,7 +42,9 @@
         ).astype(jnp.float32)
 
     def hidden_rows(share):
-        return lax.all_gather(share, "narrow", axis=0, tiled=True)
+        return jnp.concatenate(
+            lax.all_to_all(jnp.stack([share] * lax.axis_size("narrow")), "narrow", 0, 0), axis=0
+        )
 
     def width_sum(source, weight_matrices, pattern):
         amount = lax.axis_size("wide") * (token_count // wide_size)

time: 780 us -> 854 us (1.095)
  waiting for transfers between devices: 149 us -> 239 us
  local copies, waits for them, and re-layouts: 265 us -> 243 us
  starting transfers between devices: 4.92 us -> 14.4 us
    all_to_all x0 -> x2, waiting for transfers between devices: none -> 137 us  [hidden_rows(): lax.all_to_all(jnp.stack([share] * lax.axis_size('narrow')), 'narrow', 0, 0)]
    all_gather x2 -> x0, waiting for transfers between devices: 44.2 us -> none  [hidden_rows(): return lax.all_gather(share, 'narrow', axis=0, tiled=True)]
    unnamed x23, local copies, waits for them, and re-layouts: 70.7 us -> 53 us
    another operation x4, local copies, waits for them, and re-layouts: 26 us -> 10.7 us  [the longest x2 6.98 us: hidden_rows(): jnp.stack([share] * lax.axis_size('narrow'))]
    dynamic_slice x0 -> x4, local copies, waits for them, and re-layouts: none -> 9.74 us  [width_sum(): lax.map(apply_block, row_segment.reshape(amount // step_rows, step_rows,...]
    all_to_all x0 -> x2, starting transfers between devices: none -> 9.54 us  [hidden_rows(): lax.all_to_all(jnp.stack([share] * lax.axis_size('narrow')), 'narrow', 0, 0)]
    unnamed x8 -> x6, waiting for transfers between devices: 42.3 us -> 41.8 us
  transfers between devices with their start and end apart: 7 -> 7, of which waited for: 4 -> 5; matrix products, arithmetic and copies ran while one was open for 55% -> 32% of each run, Pallas kernels for 0% -> 0%
where the time goes in v1:
time: 854 us; the launch traced here: 842 us
  matrix products  254 us (30%)
  local copies, waits for them, and re-layouts  243 us (28%)
  waiting for transfers between devices  239 us (28%)
  blocking collectives  57.4 us (7%)
  starting transfers between devices  14.4 us (2%)
  between operations  14.2 us (2%)
  loops' own time  13.4 us (2%)
    all_to_all x2, waiting for transfers between devices, hidden_rows(): lax.all_to_all(jnp.stack([share] * lax.axis_size('narrow')), 'narrow', 0, 0)  137 us
    dot_general x4, matrix products, apply_block(): jnp.einsum('svob,voy->syb', lower_bound, block_selector, preferred_elemen...  62.7 us
    dot_general x4, matrix products, apply_block(): jnp.einsum('svob,voy->syb', upper_bound, block_selector, preferred_elemen...  62.6 us
    dot_general x4, matrix products, apply_block(): jnp.einsum(pattern, rows_block, weight_matrices, preferred_element_type=j...  59.1 us
    all_to_all x1, blocking collectives, on_device(): lax.all_to_all(upstream, 'narrow', split_axis=1, concat_axis=0, tiled=True)  57.4 us
    gather x2, local copies, waits for them, and re-layouts, on_device(): jnp.take(token_all.reshape(token_count, group_blocks, block_size), block_...  53 us
    unnamed x23, local copies, waits for them, and re-layouts  53 us
    gather x2, local copies, waits for them, and re-layouts, on_device(): jnp.take(upstream_all.reshape(token_count, group_blocks, block_size), blo...  52.9 us
  transfers between devices with their start and end apart: 7, of which 5 were waited for; matrix products, arithmetic and copies ran while one was open for 32% of the time, Pallas kernels for 0%

profile of v1, /device:TPU:0, one launch (start us, length us, event | category | flops | bytes accessed | tf_op | source)
XLA Modules:
  0.0 842.1 jit_solution(8306748378849916145)
XLA Ops:
  23.1 31.8 %all-to-all-done = bf16[128,8,1536]{0,2,1:T(8,128)(2,1)S(1)} async-done(((bf16[128,8,1536]{0,2,1:T(8,128)(2,1)}), bf16[128,8,1536]{0,2,1:T(8,128)(2,1)S(1)}, u32[]{:S(2)}, u32[]{:S(2)}) %all-to-all-start) | async-done | bytes 3145760 | tf_op jit(solution)/shard_map/all_to_all | solution.py:22
  86.5 40.7 %copy.63 = bf16[24,5,1024,128]{2,3,1,0:T(8,128)(2,1)} copy(bf16[24,5,1024,128]{3,2,1,0:T(8,128)(2,1)} %bitcast.164) | data formatting | bytes 62914560 | tf_op jit(solution)/shard_map/jit(_take)/gather | solution.py:26
  127.3 16.1 %bitcast_convert_fusion.3 = bf16[24,128,1024]{2,1,0:T(8,128)(2,1)} fusion(bf16[24,5,128,128]{3,2,1,0:T(8,128)(2,1)} %get-tuple-element.238, bf16[24,5,1024,128]{2,3,1,0:T(8,128)(2,1)} %copy.63, pred[24,5]{1,0:T(8,128)(4,1)S(1)} %copy.58), kind=kOutput, calls=%fused_computation.55 | convolution fusion | flops 4045406208 | bytes 41681016 | tf_op jit(solution)/shard_map/tpck,pckf->tpf/dot_general | solution.py:34
  155.6 57.4 %all_to_all.42 = bf16[128,8,1536]{0,2,1:T(8,128)(2,1)S(1)} all-to-all(bf16[128,8,1536]{0,2,1:T(8,128)(2,1)S(1)} %bitcast.176), channel_id=1, replica_groups=mesh['wide'=16,'narrow'=8] {'narrow'}, dimensions={1} | all-to-all | bytes 6291456 | tf_op jit(solution)/shard_map/all_to_all | solution.py:23
  241.0 40.7 %copy.74 = bf16[24,5,1024,128]{2,3,1,0:T(8,128)(2,1)} copy(bf16[24,5,1024,128]{3,2,1,0:T(8,128)(2,1)} %bitcast.163) | data formatting | bytes 62914560 | tf_op jit(solution)/shard_map/jit(_take)/gather | solution.py:29
  281.6 16.4 %bitcast_convert_fusion.2 = bf16[24,128,1024]{2,1,0:T(8,128)(2,1)} fusion(bf16[24,5,128,128]{3,2,1,0:T(8,128)(2,1)} %get-tuple-element.220, bf16[24,5,1024,128]{2,3,1,0:T(8,128)(2,1)} %copy.74, pred[24,5]{1,0:T(8,128)(4,1)S(1)} %copy.58), kind=kOutput, calls=%fused_computation.54 | convolution fusion | flops 4045406208 | bytes 41681016 | tf_op jit(solution)/shard_map/tpck,pcfk->tpf/dot_general | solution.py:34
  308.2 41.7 %reduce-scatter.15.cloned.1.call-done = bf16[128,3072]{1,0:T(8,128)(2,1)} async-done(((bf16[1024,3072]{1,0:T(8,128)(2,1)}), bf16[128,3072]{1,0:T(8,128)(2,1)}) %reduce-scatter.15.cloned.1.call-update) | async-done | bytes 786448
  361.6 71.9 %all-to-all-done.1 = bf16[8,128,3072]{2,1,0:T(8,128)(2,1)} async-done(((bf16[8,128,3072]{2,1,0:T(8,128)(2,1)}), bf16[8,128,3072]{2,1,0:T(8,128)(2,1)}, u32[]{:S(2)}, u32[]{:S(2)}) %all-to-all-start.1) | async-done | bytes 6291488 | tf_op jit(solution)/shard_map/all_to_all | solution.py:46
  449.2 64.7 %all-to-all-done.3 = bf16[8,128,3072]{2,1,0:T(8,128)(2,1)} async-done(((bf16[8,128,3072]{2,1,0:T(8,128)(2,1)}), bf16[8,128,3072]{2,1,0:T(8,128)(2,1)}, u32[]{:S(2)}, u32[]{:S(2)}) %all-to-all-start.3) | async-done | bytes 6291488 | tf_op jit(solution)/shard_map/all_to_all | solution.py:46
  523.2 106.2 %while.23 = (s32[]{:T(128)}, bf16[2,512,1536]{1,2,0:T(8,128)(2,1)}, bf16[2,512,24,128]{3,2,1,0:T(8,128)(2,1)}, bf16[24,5,128,128]{3,2,1,0:T(8,128)(2,1)}, s32[24,5]{0,1:T(8,128)S(1)}, /*index=5*/s32[]{:T(128)}) while((s32[]{:T(128)}, bf16[2,512,1536]{1,2,0:T(8,128)(2,1)}, bf16[2,512,24,128]{3,2,1,0:T(8,128)(2,1)}, ...), condition=%wide.region_6.8_spmd.clone, body=%wide.region_5.7_spmd.clone.sunk | while | flops 2423789056 | bytes 90441224 | solution.py:68
  540.7 15.6 %fusion.109 = f32[512,128,12,1]{1,2,3,0:T(8,128)S(1)} fusion(bf16[512,24,5,128]{3,0,2,1:T(8,128)(2,1)} %get-tuple-element.215, s32[24,5]{0,1:T(8,128)S(1)} %get-tuple-element.251), kind=kOutput, calls=%fused_computation.25.clone.1 | convolution fusion | flops 188746560 | bytes 18874848 | tf_op jit(solution)/shard_map/while/body/eval_jaxpr/svob,voy->syb/dot_general | solution.py:63
  556.3 15.6 %fusion.110 = bf16[512,12,128]{2,1,0:T(8,128)(2,1)} fusion(f32[512,128,12,1]{1,2,3,0:T(8,128)S(1)} %fusion.109, bf16[512,24,5,128]{3,0,2,1:T(8,128)(2,1)} %get-tuple-element.216, s32[24,5]{0,1:T(8,128)S(1)} %get-tuple-element.251), kind=kOutput, calls=%fused_computation.30.clone.1 | convolution fusion | flops 190319424 | bytes 20447712 | tf_op jit(solution)/shard_map/while/body/eval_jaxpr/svob,voy->syb/dot_general | solution.py:60
  593.6 15.6 %fusion.109 = f32[512,128,12,1]{1,2,3,0:T(8,128)S(1)} fusion(bf16[512,24,5,128]{3,0,2,1:T(8,128)(2,1)} %get-tuple-element.215, s32[24,5]{0,1:T(8,128)S(1)} %get-tuple-element.251), kind=kOutput, calls=%fused_computation.25.clone.1 | convolution fusion | flops 188746560 | bytes 18874848 | tf_op jit(solution)/shard_map/while/body/eval_jaxpr/svob,voy->syb/dot_general | solution.py:63
  609.2 15.6 %fusion.110 = bf16[512,12,128]{2,1,0:T(8,128)(2,1)} fusion(f32[512,128,12,1]{1,2,3,0:T(8,128)S(1)} %fusion.109, bf16[512,24,5,128]{3,0,2,1:T(8,128)(2,1)} %get-tuple-element.216, s32[24,5]{0,1:T(8,128)S(1)} %get-tuple-element.251), kind=kOutput, calls=%fused_computation.30.clone.1 | convolution fusion | flops 190319424 | bytes 20447712 | tf_op jit(solution)/shard_map/while/body/eval_jaxpr/svob,voy->syb/dot_general | solution.py:60
  636.0 119.4 %while.22 = (s32[]{:T(128)}, bf16[2,512,1536]{1,2,0:T(8,128)(2,1)}, bf16[2,512,24,128]{3,2,1,0:T(8,128)(2,1)}, bf16[24,5,128,128]{3,2,1,0:T(8,128)(2,1)}, s32[24,5]{0,1:T(8,128)S(1)}, /*index=5*/s32[]{:T(128)}) while((s32[]{:T(128)}, bf16[2,512,1536]{1,2,0:T(8,128)(2,1)}, bf16[2,512,24,128]{3,2,1,0:T(8,128)(2,1)}, ...), condition=%wide.region_2.4_spmd.clone, body=%wide.region_1.3_spmd.clone.sunk | while | flops 2423789056 | bytes 90441224 | solution.py:68
  651.3 14.9 %fusion.100 = (bf16[512,24,5,128]{3,0,2,1:T(8,128)(2,1)}, bf16[512,24,5,128]{3,0,2,1:T(8,128)(2,1)}) fusion(bf16[24,5,128,128]{3,2,1,0:T(8,128)(2,1)} %get-tuple-element.232, bf16[1,512,24,128]{3,2,1,0:T(8,128)(2,1)S(1)} %constant_dynamic-slice_fusion.4), kind=kOutput, calls=%fused_computation.6.clone.1 | convolution fusion | flops 2044723200 | bytes 38535168 | tf_op jit(solution)/shard_map/while/body/eval_jaxpr/tpf,pcfk->tpck/dot_general | solution.py:55
  666.2 15.8 %fusion.101 = f32[512,128,12,1]{1,2,3,0:T(8,128)S(1)} fusion(bf16[512,24,5,128]{3,0,2,1:T(8,128)(2,1)} %get-tuple-element.208, s32[24,5]{0,1:T(8,128)S(1)} %get-tuple-element.233), kind=kOutput, calls=%fused_computation.7.clone.1 | convolution fusion | flops 188746560 | bytes 18874848 | tf_op jit(solution)/shard_map/while/body/eval_jaxpr/svob,voy->syb/dot_general | solution.py:63
  682.0 15.7 %fusion.102 = bf16[512,12,128]{2,1,0:T(8,128)(2,1)} fusion(f32[512,128,12,1]{1,2,3,0:T(8,128)S(1)} %fusion.101, bf16[512,24,5,128]{3,0,2,1:T(8,128)(2,1)} %get-tuple-element.209, s32[24,5]{0,1:T(8,128)S(1)} %get-tuple-element.233), kind=kOutput, calls=%fused_computation.12.clone.1 | convolution fusion | flops 190319424 | bytes 20447712 | tf_op jit(solution)/shard_map/while/body/eval_jaxpr/svob,voy->syb/dot_general | solution.py:60
  704.7 14.7 %fusion.100 = (bf16[512,24,5,128]{3,0,2,1:T(8,128)(2,1)}, bf16[512,24,5,128]{3,0,2,1:T(8,128)(2,1)}) fusion(bf16[24,5,128,128]{3,2,1,0:T(8,128)(2,1)} %get-tuple-element.232, bf16[1,512,24,128]{3,2,1,0:T(8,128)(2,1)S(1)} %constant_dynamic-slice_fusion.4), kind=kOutput, calls=%fused_computation.6.clone.1 | convolution fusion | flops 2044723200 | bytes 38535168 | tf_op jit(solution)/shard_map/while/body/eval_jaxpr/tpf,pcfk->tpck/dot_general | solution.py:55
  719.4 15.6 %fusion.101 = f32[512,128,12,1]{1,2,3,0:T(8,128)S(1)} fusion(bf16[512,24,5,128]{3,0,2,1:T(8,128)(2,1)} %get-tuple-element.208, s32[24,5]{0,1:T(8,128)S(1)} %get-tuple-element.233), kind=kOutput, calls=%fused_computation.7.clone.1 | convolution fusion | flops 188746560 | bytes 18874848 | tf_op jit(solution)/shard_map/while/body/eval_jaxpr/svob,voy->syb/dot_general | solution.py:63
  735.1 15.6 %fusion.102 = bf16[512,12,128]{2,1,0:T(8,128)(2,1)} fusion(f32[512,128,12,1]{1,2,3,0:T(8,128)S(1)} %fusion.101, bf16[512,24,5,128]{3,0,2,1:T(8,128)(2,1)} %get-tuple-element.209, s32[24,5]{0,1:T(8,128)S(1)} %get-tuple-element.233), kind=kOutput, calls=%fused_computation.12.clone.1 | convolution fusion | flops 190319424 | bytes 20447712 | tf_op jit(solution)/shard_map/while/body/eval_jaxpr/svob,voy->syb/dot_general | solution.py:60
  760.1 18.6 %select_bitcast_fusion = f32[24,5,128,128]{2,3,1,0:T(8,128)} fusion(pred[24,5]{1,0:T(8,128)(4,1)S(1)} %copy-done.3, bf16[1024,24,128,1]{2,1,0,3:T(8,128)(2,1)} %bitcast.168, bf16[24,5,1024,128]{2,3,1,0:T(8,128)(2,1)} %copy.74, pred[24,5]{1,0:T(8,128)(4,1)S(1)} %copy-done.5), kind=kOutput, calls=%fused_computation.56 | convolution fusion | flops 4044226560 | bytes 45613296 | tf_op jit(solution)/shard_map/tpf,tpck->pcfk/dot_general | solution.py:90
  787.9 18.9 %broadcast_select_fusion.6 = f32[24,5,128,128]{3,2,1,0:T(8,128)} fusion(pred[24,5]{1,0:T(8,128)(4,1)S(1)} %copy-done.3, bf16[1024,24,128,1]{2,1,0,3:T(8,128)(2,1)} %bitcast.170, bf16[24,5,1024,128]{2,3,1,0:T(8,128)(2,1)} %copy.63, pred[24,5]{1,0:T(8,128)(4,1)S(1)} %copy-done.5), kind=kOutput, calls=%fused_computation.59 | convolution fusion | flops 4044226560 | bytes 45613296 | tf_op jit(solution)/shard_map/tpck,tpf->pckf/dot_general | solution.py:97
  806.8 28.6 %reduce-scatter.9.cloned.1.call-done = bf16[64,1536]{1,0:T(8,128)(2,1)} async-done(((bf16[1024,1536]{1,0:T(8,128)(2,1)}), bf16[64,1536]{1,0:T(8,128)(2,1)}) %reduce-scatter.9.cloned.1.call-update) | async-done | bytes 196624 | tf_op jit(solution)/shard_map/reduce_scatter | solution.py:71
  (75 shorter events, 212.1 us)
Async XLA Ops:
  11.8 4.7 copy-start
  11.8 5.1 copy-start.6
  11.8 43.1 %all-to-all-start = ((bf16[128,8,1536]{0,2,1:T(8,128)(2,1)}), bf16[128,8,1536]{0,2,1:T(8,128)(2,1)S(1)}, u32[]{:S(2)}, u32[]{:S(2)}) async-start(bf16[128,8,1536]{0,2,1:T(8,128)(2,1)} %bitcast.174), calls=%async_computation | async-start | bytes 6291456 | tf_op jit(solution)/shard_map/all_to_all | solution.py:22
  16.5 290.2 %reduce-scatter.13.cloned.1.call-start = ((), (), s32[]{:S(2)}) async-start(), calls=%async_computation.10 | async-start | bytes 7077888
  16.7 265.0 %copy-start.4 = (pred[24,5]{1,0:T(8,128)(4,1)}, pred[24,5]{1,0:T(8,128)(4,1)S(1)}, u32[]{:S(2)}) copy-start(pred[24,5]{1,0:T(8,128)(4,1)S(1)} %copy.58) | copy-start | bytes 364
  17.0 0.6 copy-start.2
  152.1 197.9 %reduce-scatter.15.cloned.1.call-start = ((), (), s32[]{:S(2)}) async-start(), calls=%async_computation.11 | async-start | bytes 7077888
  356.5 76.9 %all-to-all-start.1 = ((bf16[8,128,3072]{2,1,0:T(8,128)(2,1)}), bf16[8,128,3072]{2,1,0:T(8,128)(2,1)}, u32[]{:S(2)}, u32[]{:S(2)}) async-start(bf16[8,128,3072]{2,1,0:T(8,128)(2,1)} %stack.4), calls=%async_computation.1 | async-start | bytes 12582912 | tf_op jit(solution)/shard_map/all_to_all | solution.py:46
  437.0 76.9 %all-to-all-start.3 = ((bf16[8,128,3072]{2,1,0:T(8,128)(2,1)}), bf16[8,128,3072]{2,1,0:T(8,128)(2,1)}, u32[]{:S(2)}, u32[]{:S(2)}) async-start(bf16[8,128,3072]{2,1,0:T(8,128)(2,1)} %stack.5), calls=%async_computation.4 | async-start | bytes 12582912 | tf_op jit(solution)/shard_map/all_to_all | solution.py:46
  441.7 365.0 %reduce-scatter.11.cloned.1.call-start = ((), (), s32[]{:S(2)}) async-start(), calls=%async_computation.9 | async-start | bytes 3342336 | tf_op jit(solution)/shard_map/reduce_scatter | solution.py:71
  513.9 9.3 %copy-start.1 = (s32[24,5]{0,1:T(8,128)S(1)}, s32[24,5]{0,1:T(8,128)}, u32[]{:S(2)}) copy-start(s32[24,5]{0,1:T(8,128)} %param.15) | copy-start | bytes 1444
  634.0 201.3 %reduce-scatter.9.cloned.1.call-start = ((), (), s32[]{:S(2)}) async-start(), calls=%async_computation.8 | async-start | bytes 3342336 | tf_op jit(solution)/shard_map/reduce_scatter | solution.py:71
  755.4 4.7 copy-start.3
  755.4 4.7 copy-start.5
Sparse Core Ops, SparseCore 0:
  152.2 74.9 reduce-scatter.12
  306.8 43.1 reduce-scatter.14
  634.2 75.3 reduce-scatter.10
  760.2 75.0 reduce-scatter.8
